TPU v7x, 256 devices: a whole 4x4x8 slice. The times are simulated.
256 devices in a mesh: aux: 16 (over y_lo, z), row: 16 (over x, y_hi, core).
Axes of the slice: x: 4, y: 4 (y_hi: 2, y_lo: 2; y = y_hi * 2 + y_lo), z: 8, core: 2. Of those that a mesh axis runs over, the one named last changes fastest.
Arguments:
- three_index: float32 [192, 2048, 512], P('aux', 'row'), may hold values from -0.40296373 to 0.40296373
- coefficients: float32 [2048, 256], P('aux'), may hold values from -0.25 to 0.25
- tile_index: int32 [16, 16, 4], P('aux', 'row'), may hold values from 0 to 15, as said below
Outputs:
- exchange_matrix: float32 [2048, 2048], P('row', 'aux')
Inputs may be any that keep to these rules, and one draw needn't show every extreme that they name: `tile_index`: the 4 tiles of one block are distinct.
All inputs are finite; a program needn't handle non-finite values.
Results may differ from a plain program's by a relative error of at most 0.00005.
Values sent between devices are 32-bit elements; how exact they have to be, the bound alone decides.
A program may use at most 128 MiB of HBM per device.

v0:
```python
import jax
import jax.numpy as jnp
from jax import lax
from jax.sharding import PartitionSpec as P

NOCC = 256
TILE = 128
NT = 4


def pair_block(left, right):
    return jnp.einsum("pmi,pni->mn", left, right, precision=lax.Precision.HIGHEST)


def on_device(three_index, coefficients, tile_index):
    all_coeff = lax.all_gather(coefficients, "aux", axis=0, tiled=True)
    tiles = tile_index.reshape(NT)
    chosen = jnp.concatenate(
        [lax.dynamic_slice_in_dim(all_coeff, tiles[slot] * TILE, TILE, 0) for slot in range(NT)],
        axis=0,
    )
    aux_rows, mu_rows, width = three_index.shape
    half = jnp.dot(
        three_index.reshape(aux_rows * mu_rows, width),
        chosen,
        precision=lax.Precision.HIGHEST,
        preferred_element_type=jnp.float32,
    ).reshape(aux_rows, mu_rows, NOCC)
    partial_rows = pair_block(half, lax.all_gather(half, "row", axis=1, tiled=True))
    return lax.psum_scatter(partial_rows, "aux", scatter_dimension=1, tiled=True)


def solution(mesh):
    return jax.shard_map(
        on_device,
        mesh=mesh,
        in_specs=(P("aux", "row", None), P("aux", None), P("aux", "row", None)),
        out_specs=P("row", "aux"),
        check_vma=False,
    )
```

profile of v0, /device:TPU:56, one launch (start us, length us, event | category | flops | bytes accessed | tf_op | source)
XLA Modules:
  0.0 349.7 jit_solution(14427937119642510914)
XLA Ops:
  6.5 0.0 copy-start
  6.5 0.0 all-gather.3.cloned.1.call-start
  6.5 0.7 all-gather.3.cloned.1.call-update
  7.3 0.0 all-gather.5.cloned.1.call-start
  7.3 1.5 fusion.8
  11.4 70.0 %all-gather.3.cloned.1.call-done = f32[2048,256]{1,0:T(8,128)} async-done(((f32[128,256]{1,0:T(8,128)}), f32[2048,256]{1,0:T(8,128)}) %all-gather.3.cloned.1.call-update) | async-done | bytes 2097168 | tf_op jit(solution)/shard_map/all_gather | solution.py:16
  81.3 1.1 constant_dynamic-slice_fusion.3
  82.5 0.0 copy-done
  82.5 6.5 %convolution_bitcast_fusion = f32[1536,256]{0,1:T(8,128)} fusion(f32[1536,512]{1,0:T(8,128)S(1)} %bitcast.13, f32[128,256]{1,0:T(8,128)S(1)} %get-tuple-element.6, f32[128,256]{1,0:T(8,128)S(1)} %get-tuple-element.7, f32[128,256]{1,0:T(8,128)S(1)} %get-tuple-element.8, f32[128,256]{1,0:T(8,128)S(1)} %get-tuple-element.5), kind=kOutput, calls=%fused_computation | convolution fusion | flops 2416312320 | bytes 5242880 | tf_op jit(solution)/shard_map/dot_general | solution.py:23
  89.0 3.1 copy.6
  92.1 0.0 all-gather.5.cloned.1.call-update
  92.1 0.2 reduce-scatter.2.cloned.1.call-start
  92.3 151.3 %all-gather.5.cloned.1.call-done = f32[12,2048,256]{2,1,0:T(8,128)} async-done(((f32[12,128,256]{2,1,0:T(8,128)}), f32[12,2048,256]{2,1,0:T(8,128)}) %all-gather.5.cloned.1.call-update) | async-done | bytes 25165840 | tf_op jit(solution)/shard_map/all_gather | solution.py:29
  243.7 31.6 %convolution_bitcast_fusion.1 = f32[128,2048]{1,0:T(8,128)} fusion(f32[12,128,256]{2,1,0:T(8,128)} %bitcast.15, f32[12,2048,256]{2,1,0:T(8,128)} %all-gather.5.cloned.1.call-done), kind=kOutput, calls=%fused_computation.1 | convolution fusion | flops 9663676416 | bytes 27787264 | tf_op jit(solution)/shard_map/pmi,pni->mn/dot_general | solution.py:12
  275.2 0.0 reduce-scatter.2.cloned.1.call-update
  275.2 68.0 %reduce-scatter.2.cloned.1.call-done = f32[128,128]{1,0:T(8,128)} async-done(((f32[128,2048]{1,0:T(8,128)}), f32[128,128]{1,0:T(8,128)}) %reduce-scatter.2.cloned.1.call-update) | async-done | bytes 65552 | tf_op jit(solution)/shard_map/reduce_scatter | solution.py:30
Async XLA Ops:
  6.5 75.9 %copy-start = (f32[12,128,512]{2,1,0:T(8,128)S(1)}, f32[12,128,512]{2,1,0:T(8,128)}, u32[]{:S(2)}) copy-start(f32[12,128,512]{2,1,0:T(8,128)} %param.3) | copy-start | bytes 9437188
  6.5 74.8 %all-gather.3.cloned.1.call-start = ((), (), s32[]{:S(2)}) async-start(), calls=%async_computation.1 | async-start | bytes 2228224 | tf_op jit(solution)/shard_map/all_gather | solution.py:16
  7.3 236.4 %all-gather.5.cloned.1.call-start = ((), (), s32[]{:S(2)}) async-start(), calls=%async_computation.2 | async-start | bytes 26738688 | tf_op jit(solution)/shard_map/all_gather | solution.py:29
  92.1 251.1 %reduce-scatter.2.cloned.1.call-start = ((), (), s32[]{:S(2)}) async-start(), calls=%async_computation.3 | async-start | bytes 1114112 | tf_op jit(solution)/shard_map/reduce_scatter | solution.py:30
Sparse Core Ops, SparseCore 0:
  9.1 72.1 all-gather.2
  92.2 151.4 all-gather.4
  275.4 67.7 reduce-scatter.1
where the time goes:
time: 354 us; the launch traced here: 350 us
  waiting for transfers between devices  290 us (82%)
  matrix products  38.1 us (11%)
  between operations  15.6 us (4%)
  local copies, waits for them, and re-layouts  5.75 us (2%)
    all_gather x1, waiting for transfers between devices, on_device(): lax.all_gather(half, 'row', axis=1, tiled=True)  151 us
    all_gather x1, waiting for transfers between devices, on_device(): all_coeff = lax.all_gather(coefficients, 'aux', axis=0, tiled=True)  70 us
    reduce_scatter x1, waiting for transfers between devices, on_device(): lax.psum_scatter(partial_rows, 'aux', scatter_dimension=1, tiled=True)  68 us
    dot_general x1, matrix products, pair_block(): jnp.einsum('pmi,pni->mn', left, right, precision=lax.Precision.HIGHEST)  31.6 us
  transfers between devices with their start and end apart: 3, of which 3 were waited for; matrix products, arithmetic and copies ran while one was open for 0% of the time, Pallas kernels for 0%

commit v1 on v0

v1 whole, which is shorter than its diff:
```python
import functools

import jax
import jax.numpy as jnp
from jax import lax
from jax.experimental import pallas as pl
from jax.experimental.pallas import tpu as pltpu
from jax.sharding import PartitionSpec as P

MESH = pl.DeviceIdType.MESH
F32 = jnp.float32
BF16 = jnp.bfloat16
NT_DIMS = (((1,), (1,)), ((), ()))
NN_DIMS = (((1,), (0,)), ((), ()))


def split(value):
    high = value.astype(BF16)
    return high, (value - high.astype(F32)).astype(BF16)


def dot3(lh, ll, rh, rl, dims):
    dot = functools.partial(lax.dot_general, dimension_numbers=dims, preferred_element_type=F32)
    return dot(lh, rh) + (dot(lh, rl) + dot(ll, rh))


def kernel(
    x_ref, c_ref, t_ref, out_ref,
    xh, xl, tslice, tvec, tall, tsm, picks, csel, ch, cl,
    hb, blk, xfull, xhalf, gg, eh, part, ry, summed, rz, red, fin,
    c1s, c1r, tis, tir, c2s, c2r, tsem, has, har, xs, xr, rys, ryr, rzs, rzr, fs, fr,
):
    a = lax.axis_index("aux")
    r = lax.axis_index("row")
    lo, z = a // 8, a % 8
    x, i = r // 4, r % 4
    hi, c = i // 2, i % 2
    y = hi * 2 + lo

    def at(px, py, pz, pc):
        return (py % 2) * 8 + pz, px * 4 + (py // 2) * 2 + pc

    def remote(src, dst, ss, rs, dev):
        return pltpu.make_async_remote_copy(
            src_ref=src, dst_ref=dst, send_sem=ss, recv_sem=rs, device_id=dev, device_id_type=MESH
        )

    def is_me(dev):
        return (dev[0] == a) & (dev[1] == r)

    e = z % 2
    bi, bj = y, z // 2
    fa_row = lax.rem(x + 4 - c, 4)
    fa_col = lax.rem(fa_row + 1, 4)
    ea, eb = lax.rem(x + 3, 4), lax.rem(x + 1, 4)
    outgoing = [
        (0, 0, (x * 4 + bj, x * 4 + bi)),
        (1, 0, (fa_col * 4 + bj, fa_row * 4 + bi)),
        (1, 1, (fa_row * 4 + bi, fa_col * 4 + bj)),
        (2, 0, (eb * 4 + bj, ea * 4 + bi)),
        (2, 1, (ea * 4 + bi, eb * 4 + bj)),
    ]
    xc, jc = a // 4, a % 4
    delta = lax.rem(xc + 4 - x, 4)
    has_plain = delta <= 2
    has_turned = delta >= 2
    incoming = []
    for sc in (0, 1):
        plain_x = jnp.where(delta == 0, x, jnp.where(delta == 1, x if sc == 0 else xc, lax.rem(x + 1, 4)))
        turned_x = jnp.where(delta == 3, xc if sc == 0 else x, lax.rem(x + 3, 4))
        for se in (0, 1):
            incoming.append((0, sc, se, has_plain, at(plain_x, i, 2 * jc + se, sc)))
            incoming.append((1, sc, se, has_turned, at(turned_x, jc, 2 * i + se, sc)))

    barrier = pltpu.get_barrier_semaphore()

    def greet(dev):
        pl.semaphore_signal(barrier, inc=1, device_id=dev, device_id_type=MESH)

    def greet_axes(d, _):
        greet((a, lax.rem(r + d, 16)))
        greet((lax.rem(a + d, 16), r))
        return 0

    lax.fori_loop(1, 16, greet_axes, 0)
    greet(at(x, 3 - y, z, c))
    for _, _, _, there, dev in incoming:
        @pl.when(there & jnp.logical_not(is_me(dev)))
        def _():
            greet(dev)
    expect = 31
    for _, _, dev in outgoing:
        expect = expect + jnp.where(is_me(dev), 0, 1)

    lane = lax.broadcasted_iota(jnp.int32, (8, 128), 1)
    ids = jnp.zeros((8, 128), jnp.int32)
    for s in range(4):
        ids = jnp.where(lane == s, t_ref[0, 0, s], ids)
    tvec[...] = ids
    pl.semaphore_wait(barrier, expect)

    def c1(d):
        return remote(c_ref.at[lax.rem(r, 16)], tslice.at[a], c1s.at[d - 1], c1r.at[d - 1], (lax.rem(a + d, 16), r))

    def c1_in(d):
        return remote(c_ref.at[r], tslice.at[lax.rem(a + 16 - d, 16)], c1s.at[d - 1], c1r.at[d - 1], (a, r))

    def ti(d):
        return remote(tvec, tall.at[r], tis.at[d - 1], tir.at[d - 1], (a, lax.rem(r + d, 16)))

    def ti_in(d):
        return remote(tvec, tall.at[lax.rem(r + 16 - d, 16)], tis.at[d - 1], tir.at[d - 1], (a, r))

    def start1(d, _):
        c1(d).start()
        ti(d).start()
        return 0

    lax.fori_loop(1, 16, start1, 0)
    tslice[a] = c_ref[r]
    tall[r] = ids

    def split_x(n, _):
        rows = pl.ds(pl.multiple_of(n * 128, 128), 128)
        high, low = split(x_ref[rows, :])
        xh[rows, :] = high
        xl[rows, :] = low
        return 0

    lax.fori_loop(0, 12, split_x, 0)

    def wait1(d, _):
        ti_in(d).wait_recv()
        return 0

    lax.fori_loop(1, 16, wait1, 0)
    to_smem = pltpu.make_async_copy(tall.at[:, 0], tsm, tsem)
    to_smem.start()
    to_smem.wait()

    def wait1c(d, _):
        c1_in(d).wait_recv()
        return 0

    lax.fori_loop(1, 16, wait1c, 0)

    def c2(d):
        return remote(picks.at[d - 1], csel.at[:, r], c2s.at[d - 1], c2r.at[d - 1], (a, lax.rem(r + d, 16)))

    def c2_in(d):
        return remote(picks.at[d - 1], csel.at[:, lax.rem(r + 16 - d, 16)], c2s.at[d - 1], c2r.at[d - 1], (a, r))

    def start2(d, _):
        who = lax.rem(r + d, 16)
        for s in range(4):
            picks[d - 1, s] = tslice[tsm[who, s]]
        c2(d).start()
        return 0

    lax.fori_loop(1, 16, start2, 0)
    for s in range(4):
        csel[s, r] = tslice[tsm[r, s]]

    def wait2(d, _):
        c2_in(d).wait_recv()
        return 0

    lax.fori_loop(1, 16, wait2, 0)
    for s in range(4):
        high, low = split(csel[s].reshape(128, 256))
        ch[s * 128:(s + 1) * 128, :] = high
        cl[s * 128:(s + 1) * 128, :] = low

    peers = [lax.rem(i + 2, 4), 3 - i, i + 1 - 2 * c]

    def swap(k):
        return remote(hb.at[k], blk.at[:, i], has.at[k], har.at[k], (a, x * 4 + peers[k]))

    def swap_in(k):
        return remote(hb.at[k], blk.at[:, peers[k]], has.at[k], har.at[k], (a, r))

    def half_of(g):
        rows = pl.ds(pl.multiple_of(g * 384, 128), 384)
        return dot3(xh[rows, :], xl[rows, :], ch[...], cl[...], NN_DIMS)

    for k in range(3):
        value = half_of(peers[k])
        for q in range(6):
            hb[k, q] = value[(q // 2) * 128:(q // 2 + 1) * 128, (q % 2) * 128:(q % 2 + 1) * 128]
        swap(k).start()
    value = half_of(i)
    for q in range(6):
        blk[q, i] = value[(q // 2) * 128:(q // 2 + 1) * 128, (q % 2) * 128:(q % 2 + 1) * 128]

    step = 2 * c - 1
    x_to = lax.rem(x + 4 + step, 4)
    x_back = lax.rem(x + 4 - step, 4)
    mine = x // 2
    others = x_to // 2

    def xsend(p, k, m):
        first = 3 * (1 - mine)
        second = 3 * mine
        if m == 0:
            return remote(blk.at[pl.ds(first, 3), p], xfull.at[pl.ds(first, 3), p], xs.at[k, 0], xr.at[k, 0], (a, x_to * 4 + i))
        if m == 1:
            return remote(blk.at[pl.ds(second, 3), p], xhalf.at[:, p], xs.at[k, 1], xr.at[k, 1], (a, x_back * 4 + i))
        return remote(blk.at[pl.ds(second, 3), p], xfull.at[pl.ds(second, 3), p], xs.at[k, 2], xr.at[k, 2], (a, x_to * 4 + i))

    def xrecv(p, k, m):
        first = 3 * others
        second = 3 * (1 - others)
        if m == 0:
            return remote(blk.at[pl.ds(first, 3), p], xfull.at[pl.ds(first, 3), p], xs.at[k, 0], xr.at[k, 0], (a, r))
        if m == 1:
            return remote(blk.at[pl.ds(0, 3), p], xhalf.at[:, p], xs.at[k, 1], xr.at[k, 1], (a, r))
        return remote(blk.at[pl.ds(second, 3), p], xfull.at[pl.ds(second, 3), p], xs.at[k, 2], xr.at[k, 2], (a, r))

    pieces = [(i, 3), (peers[2], 2), (peers[0], 0), (peers[1], 1)]
    for p, k in pieces:
        if k != 3:
            swap_in(k).wait_recv()
        for m in range(3):
            xsend(p, k, m).start()

    def turn(src, slot):
        def body(n, _):
            rows = pl.ds(pl.multiple_of(n * 128, 128), 128)
            for q in range(6):
                high, low = split(src[q, n])
                gg[slot, 0, rows, q * 128:(q + 1) * 128] = high
                gg[slot, 1, rows, q * 128:(q + 1) * 128] = low
            return 0
        lax.fori_loop(0, 4, body, 0)

    def turn_half(src, start, slot):
        def body(n, _):
            rows = pl.ds(pl.multiple_of(n * 128, 128), 128)
            for q in range(3):
                high, low = split(src[start + q, n])
                eh[slot, 0, rows, q * 128:(q + 1) * 128] = high
                eh[slot, 1, rows, q * 128:(q + 1) * 128] = low
            return 0
        lax.fori_loop(0, 4, body, 0)

    def products(t, buf, left, right):
        for jj in range(2):
            cols = slice(jj * 256, (jj + 1) * 256)
            value = dot3(buf[left, 0], buf[left, 1], buf[right, 0, cols, :], buf[right, 1, cols, :], NT_DIMS)
            for n in range(4):
                for jl in range(2):
                    for h in range(2):
                        part[t, n, (2 * jj + jl) * 2 + h] = value[
                            n * 128 + h * 64:n * 128 + (h + 1) * 64, jl * 128:(jl + 1) * 128
                        ]

    def ysend(t, d):
        py = lax.rem(y + d, 4)
        return remote(part.at[t, py], ry.at[t, d - 1], rys.at[t, d - 1], ryr.at[t, d - 1], at(x, py, z, c))

    def zsend(t, d):
        pz = lax.rem(z + d, 8)
        return remote(summed.at[t, pz], rz.at[t, d - 1], rzs.at[t, d - 1], rzr.at[t, d - 1], at(x, y, pz, c))

    def y_start(t):
        for d in (2, 1, 3):
            ysend(t, d).start()

    def y_done(t):
        for d in (1, 2, 3):
            ysend(t, d).wait_recv()
        summed[t] = part[t, y] + ry[t, 0] + ry[t, 1] + ry[t, 2]
        for d in (4, 3, 5, 2, 6, 1, 7):
            zsend(t, d).start()

    def z_done(t):
        for d in range(1, 8):
            zsend(t, d).wait_recv()
        total = summed[t, z]
        for d in range(7):
            total = total + rz[t, d]
        red[t] = total

    def deliver(n):
        t, turned, dev = outgoing[n]
        return remote(red.at[t], fin.at[turned, c, e], fs.at[n], fr.at[turned, c, e], dev)

    def send_out(n):
        t, turned, dev = outgoing[n]

        @pl.when(jnp.logical_not(is_me(dev)))
        def _():
            deliver(n).start()

        @pl.when(is_me(dev))
        def _():
            fin[turned, c, e] = red[t]

    turn(blk, c)
    products(0, gg, c, c)
    y_start(0)
    for p, k in pieces:
        xrecv(p, k, 0).wait_recv()
        xrecv(p, k, 1).wait_recv()
    turn_half(xhalf, 0, c)
    turn_half(xfull, 3 * others, 1 - c)
    products(2, eh, 0, 1)
    y_start(2)
    y_done(0)
    for p, k in pieces:
        xrecv(p, k, 2).wait_recv()
    turn(xfull, 1 - c)
    products(1, gg, 0, 1)
    y_start(1)
    y_done(2)
    z_done(0)
    send_out(0)
    y_done(1)
    z_done(2)
    send_out(3)
    send_out(4)
    z_done(1)
    send_out(1)
    send_out(2)

    for turned, sc, se, there, dev in incoming:
        @pl.when(there & jnp.logical_not(is_me(dev)))
        def _():
            remote(red.at[0], fin.at[turned, sc, se], fs.at[0], fr.at[turned, sc, se], (a, r)).wait_recv()

    def gathered(turned):
        return (fin[turned, 0] + fin[turned, 1]).reshape(128, 128)

    @pl.when(delta <= 1)
    def _():
        out_ref[...] = gathered(0)

    @pl.when(delta == 2)
    def _():
        out_ref[...] = gathered(0) + gathered(1).T

    @pl.when(delta == 3)
    def _():
        out_ref[...] = gathered(1).T

    def drain(d, _):
        c1(d).wait_send()
        ti(d).wait_send()
        c2(d).wait_send()
        return 0

    lax.fori_loop(1, 16, drain, 0)
    for k in range(3):
        swap(k).wait_send()
    for p, k in pieces:
        for m in range(3):
            xsend(p, k, m).wait_send()
    for t in range(3):
        for d in range(1, 4):
            ysend(t, d).wait_send()
        for d in range(1, 8):
            zsend(t, d).wait_send()
    for n in range(5):
        @pl.when(jnp.logical_not(is_me(outgoing[n][2])))
        def _():
            deliver(n).wait_send()


def on_device(three_index, coefficients, tile_index):
    dma = pltpu.SemaphoreType.DMA
    vm = pltpu.VMEM
    return pl.pallas_call(
        kernel,
        out_shape=jax.ShapeDtypeStruct((128, 128), F32),
        in_specs=[
            pl.BlockSpec(memory_space=pltpu.VMEM),
            pl.BlockSpec(memory_space=pltpu.VMEM),
            pl.BlockSpec(memory_space=pltpu.SMEM),
        ],
        out_specs=pl.BlockSpec(memory_space=pltpu.VMEM),
        scratch_shapes=[
            vm((1536, 512), BF16), vm((1536, 512), BF16),
            vm((16, 8, 256), F32), vm((8, 128), jnp.int32), vm((16, 8, 128), jnp.int32),
            pltpu.SMEM((16, 128), jnp.int32),
            vm((15, 4, 8, 256), F32), vm((4, 16, 8, 256), F32),
            vm((512, 256), BF16), vm((512, 256), BF16),
            vm((3, 6, 128, 128), F32), vm((6, 4, 128, 128), F32), vm((6, 4, 128, 128), F32), vm((3, 4, 128, 128), F32),
            vm((2, 2, 512, 768), BF16), vm((2, 2, 512, 384), BF16),
            vm((3, 4, 8, 64, 128), F32), vm((3, 3, 8, 64, 128), F32), vm((3, 8, 64, 128), F32),
            vm((3, 7, 64, 128), F32), vm((3, 64, 128), F32), vm((2, 2, 2, 64, 128), F32),
            dma((15,)), dma((15,)), dma((15,)), dma((15,)), dma((15,)), dma((15,)), dma,
            dma((3,)), dma((3,)), dma((4, 3)), dma((4, 3)),
            dma((3, 3)), dma((3, 3)), dma((3, 7)), dma((3, 7)), dma((5,)), dma((2, 2, 2)),
        ],
        compiler_params=pltpu.CompilerParams(
            collective_id=0, has_side_effects=True, vmem_limit_bytes=56 * 2**20
        ),
    )(three_index.reshape(1536, 512), coefficients.reshape(16, 8, 256), tile_index)


def solution(mesh):
    return jax.shard_map(
        on_device,
        mesh=mesh,
        in_specs=(P("aux", "row", None), P("aux", None), P("aux", "row", None)),
        out_specs=P("row", "aux"),
        check_vma=False,
    )
```

time: 354 us -> 110 us (0.31)
  the two profiles are of different devices: /device:TPU:56 before, /device:TPU:18 now
where the time goes in v1:
time: 110 us
  Pallas kernels  108 us (98%)
  local copies, waits for them, and re-layouts  1.47 us (1%)
    pallas_call x1, Pallas kernels, on_device(): pl.pallas_call(kernel, out_shape=jax.ShapeDtypeStruct((128, 128), F32), i...  108 us

profile of v1, /device:TPU:18, one launch (start us, length us, event | category | flops | bytes accessed | tf_op | source)
XLA Modules:
  0.0 109.7 jit_solution(11983622538484621940)
XLA Ops:
  0.0 108.2 %shard_map.37 = f32[128,128]{1,0:T(8,128)} custom-call(f32[1536,512]{1,0:T(8,128)} %bitcast.2, f32[16,8,256]{2,1,0:T(8,128)} %bitcast.3, s32[1,1,4]{2,1,0:T(1,128)} %t_ref.1), custom_call_target="tpu_custom_call" | custom-call | tf_op jit(solution)/shard_map/pallas_call | solution.py:372
  108.2 1.5 %copy.5 = f32[128,128]{1,0:T(8,128)} copy(f32[128,128]{1,0:T(8,128)} %shard_map.37) | data formatting | bytes 131072

commit v2 on v1

v2 whole, which is shorter than its diff:
```python
import functools

import jax
import jax.numpy as jnp
from jax import lax
from jax.experimental import pallas as pl
from jax.experimental.pallas import tpu as pltpu
from jax.sharding import PartitionSpec as P

MESH = pl.DeviceIdType.MESH
F32 = jnp.float32
BF16 = jnp.bfloat16
NT_DIMS = (((1,), (1,)), ((), ()))
NN_DIMS = (((1,), (0,)), ((), ()))


def split(value):
    high = value.astype(BF16)
    return high, (value - high.astype(F32)).astype(BF16)


def dot3(lh, ll, rh, rl, dims):
    dot = functools.partial(lax.dot_general, dimension_numbers=dims, preferred_element_type=F32)
    return dot(lh, rh) + (dot(lh, rl) + dot(ll, rh))


def kernel(
    x_ref, c_ref, t_ref, out_ref,
    xv, xh, xl, tslice, tvec, tall, tsm, picks, csel, ch, cl,
    hb, blk, xfull, xhalf, gg, eh,
    pc, cb, pf, ryf, sf, rzf, redf, rye, se_, rze, rzd, sd, ryd, redq, fin_q, fin_f,
    loads, c1s, c1r, tis, tir, c2s, c2r, tsem, has, har, xs, xr, ccs, ccr,
    fys, fyr, fzs, fzr, eys, eyr, ezs, ezr, dys, dyr, dzs, dzr, fs, frq, frf,
):
    a = lax.axis_index("aux")
    r = lax.axis_index("row")
    lo, z = a // 8, a % 8
    x, i = r // 4, r % 4
    hi, c = i // 2, i % 2
    y = hi * 2 + lo

    def at(px, py, pz, pc):
        return (py % 2) * 8 + pz, px * 4 + (py // 2) * 2 + pc

    def remote(src, dst, ss, rs, dev):
        return pltpu.make_async_remote_copy(
            src_ref=src, dst_ref=dst, send_sem=ss, recv_sem=rs, device_id=dev, device_id_type=MESH
        )

    def is_me(dev):
        return (dev[0] == a) & (dev[1] == r)

    def load_x(n):
        return pltpu.make_async_copy(x_ref.at[pl.ds(n * 384, 384)], xv.at[pl.ds(n * 384, 384)], loads.at[n])

    for n in range(4):
        load_x(n).start()

    sub = z % 2
    bi, bj = y, z // 2
    step = 2 * c - 1
    x_to = lax.rem(x + 4 + step, 4)
    x_back = lax.rem(x + 4 - step, 4)
    ea, eb = lax.rem(x + 3, 4), lax.rem(x + 1, 4)
    outgoing = [
        ((x * 4 + bj, x * 4 + bi), redq.at[0], fin_q.at[0, c, sub], frq.at[0, c, sub]),
        ((x_back * 4 + bj, x * 4 + bi), redf, fin_f.at[0, sub], frf.at[0, sub]),
        ((x * 4 + bi, x_back * 4 + bj), redf, fin_f.at[1, sub], frf.at[1, sub]),
        ((eb * 4 + bj, ea * 4 + bi), redq.at[1], fin_q.at[0, c, sub], frq.at[0, c, sub]),
        ((ea * 4 + bi, eb * 4 + bj), redq.at[1], fin_q.at[1, c, sub], frq.at[1, c, sub]),
    ]
    xc, jc = a // 4, a % 4
    delta = lax.rem(xc + 4 - x, 4)
    even = (delta % 2) == 0
    odd = (delta % 2) == 1
    turned = delta == 2
    near = delta // 2
    incoming = []
    for n in (0, 1):
        for k in (0, 1):
            incoming.append((even, at(lax.rem(x + near, 4), i, 2 * jc + n, k), fin_q.at[0, k, n], frq.at[0, k, n], redq.at[0]))
            incoming.append((turned, at(lax.rem(x + 3, 4), jc, 2 * i + n, k), fin_q.at[1, k, n], frq.at[1, k, n], redq.at[0]))
        incoming.append((odd, at(x, i, 2 * jc + n, near), fin_f.at[0, n], frf.at[0, n], redf))
        incoming.append((odd, at(xc, jc, 2 * i + n, 1 - near), fin_f.at[1, n], frf.at[1, n], redf))

    barrier = pltpu.get_barrier_semaphore()

    def greet(dev):
        pl.semaphore_signal(barrier, inc=1, device_id=dev, device_id_type=MESH)

    def greet_axes(d, _):
        greet((a, lax.rem(r + d, 16)))
        greet((lax.rem(a + d, 16), r))
        return 0

    lax.fori_loop(1, 16, greet_axes, 0)
    greet(at(x, 3 - y, z, c))
    for there, dev, _, _, _ in incoming:
        @pl.when(there & jnp.logical_not(is_me(dev)))
        def _():
            greet(dev)
    expect = 31
    for dev, _, _, _ in outgoing:
        expect = expect + jnp.where(is_me(dev), 0, 1)

    lane = lax.broadcasted_iota(jnp.int32, (8, 128), 1)
    ids = jnp.zeros((8, 128), jnp.int32)
    for s in range(4):
        ids = jnp.where(lane == s, t_ref[0, 0, s], ids)
    tvec[...] = ids
    pl.semaphore_wait(barrier, expect)

    def c1(d):
        return remote(c_ref.at[r], tslice.at[a], c1s.at[d - 1], c1r.at[d - 1], (lax.rem(a + d, 16), r))

    def c1_in(d):
        return remote(c_ref.at[r], tslice.at[lax.rem(a + 16 - d, 16)], c1s.at[d - 1], c1r.at[d - 1], (a, r))

    def ti(d):
        return remote(tvec, tall.at[r], tis.at[d - 1], tir.at[d - 1], (a, lax.rem(r + d, 16)))

    def ti_in(d):
        return remote(tvec, tall.at[lax.rem(r + 16 - d, 16)], tis.at[d - 1], tir.at[d - 1], (a, r))

    def start1(d, _):
        c1(d).start()
        ti(d).start()
        return 0

    lax.fori_loop(1, 16, start1, 0)
    tslice[a] = c_ref[r]
    tall[r] = ids

    def split_x(n, _):
        rows = pl.ds(pl.multiple_of(n * 128, 128), 128)
        high, low = split(xv[rows, :])
        xh[rows, :] = high
        xl[rows, :] = low
        return 0

    for n in range(4):
        load_x(n).wait()
    lax.fori_loop(0, 12, split_x, 0)

    def wait1(d, _):
        ti_in(d).wait_recv()
        return 0

    lax.fori_loop(1, 16, wait1, 0)
    to_smem = pltpu.make_async_copy(tall.at[:, 0], tsm, tsem)
    to_smem.start()
    to_smem.wait()

    def wait1c(d, _):
        c1_in(d).wait_recv()
        return 0

    lax.fori_loop(1, 16, wait1c, 0)

    def c2(d):
        return remote(picks.at[d - 1], csel.at[:, r], c2s.at[d - 1], c2r.at[d - 1], (a, lax.rem(r + d, 16)))

    def c2_in(d):
        return remote(picks.at[d - 1], csel.at[:, lax.rem(r + 16 - d, 16)], c2s.at[d - 1], c2r.at[d - 1], (a, r))

    def start2(d, _):
        who = lax.rem(r + d, 16)
        for s in range(4):
            picks[d - 1, s] = tslice[tsm[who, s]]
        c2(d).start()
        return 0

    lax.fori_loop(1, 16, start2, 0)
    for s in range(4):
        csel[s, r] = tslice[tsm[r, s]]

    def wait2(d, _):
        c2_in(d).wait_recv()
        return 0

    lax.fori_loop(1, 16, wait2, 0)
    for s in range(4):
        high, low = split(csel[s].reshape(128, 256))
        ch[s * 128:(s + 1) * 128, :] = high
        cl[s * 128:(s + 1) * 128, :] = low

    peers = [lax.rem(i + 2, 4), 3 - i, i + 1 - 2 * c]

    def swap(k):
        return remote(hb.at[k], blk.at[:, i], has.at[k], har.at[k], (a, x * 4 + peers[k]))

    def swap_in(k):
        return remote(hb.at[k], blk.at[:, peers[k]], has.at[k], har.at[k], (a, r))

    def half_of(g):
        rows = pl.ds(pl.multiple_of(g * 384, 128), 384)
        return dot3(xh[rows, :], xl[rows, :], ch[...], cl[...], NN_DIMS)

    def chunk(value, q):
        return value[(q // 2) * 128:(q // 2 + 1) * 128, (q % 2) * 128:(q % 2 + 1) * 128]

    def turn(src, slot, p):
        rows = pl.ds(pl.multiple_of(p * 128, 128), 128)
        for q in range(6):
            high, low = split(src[q, p])
            gg[slot, 0, rows, q * 128:(q + 1) * 128] = high
            gg[slot, 1, rows, q * 128:(q + 1) * 128] = low

    def turn_half(src, start, slot):
        def body(n, _):
            rows = pl.ds(pl.multiple_of(n * 128, 128), 128)
            for q in range(3):
                high, low = split(src[start + q, n])
                eh[slot, 0, rows, q * 128:(q + 1) * 128] = high
                eh[slot, 1, rows, q * 128:(q + 1) * 128] = low
            return 0
        lax.fori_loop(0, 4, body, 0)

    mine = x // 2
    others = x_to // 2

    def whole(p, k):
        return remote(blk.at[:, p], xfull.at[:, p], xs.at[k, 0], xr.at[k, 0], (a, x_to * 4 + i))

    def part_way(p, k):
        return remote(blk.at[pl.ds(3 * mine, 3), p], xhalf.at[:, p], xs.at[k, 1], xr.at[k, 1], (a, x_back * 4 + i))

    def square(n, buf, left, right):
        for jj in range(2):
            cols = slice(jj * 256, (jj + 1) * 256)
            value = dot3(buf[left, 0], buf[left, 1], buf[right, 0, cols, :], buf[right, 1, cols, :], NT_DIMS)
            for m in range(4):
                for jl in range(2):
                    for h in range(2):
                        pc[n, h, m, 2 * jj + jl] = value[
                            m * 128 + h * 64:m * 128 + (h + 1) * 64, jl * 128:(jl + 1) * 128
                        ].reshape(2, 32, 128)

    def core_swap(n):
        return remote(pc.at[n, 1 - c], cb.at[n], ccs.at[n], ccr.at[n], (a, r + 1 - 2 * c))

    def core_sum(n):
        core_swap(n).wait_recv()
        for m in range(4):
            pc[n, c, m] = pc[n, c, m] + cb[n, m]

    def fy(d, p):
        py = lax.rem(y + d, 4)
        return remote(pf.at[py, p], ryf.at[d - 1, p], fys.at[p, d - 1], fyr.at[p, d - 1], at(x, py, z, c))

    def fz(d):
        pz = lax.rem(z + d, 8)
        return remote(sf.at[pz], rzf.at[d - 1], fzs.at[d - 1], fzr.at[d - 1], at(x, y, pz, c))

    def ey(d):
        py = lax.rem(y + d, 4)
        return remote(pc.at[1, c, py], rye.at[d - 1], eys.at[d - 1], eyr.at[d - 1], at(x, py, z, c))

    def ez(d):
        pz = lax.rem(z + d, 8)
        return remote(se_.at[pz // 2, pz % 2], rze.at[d - 1], ezs.at[d - 1], ezr.at[d - 1], at(x, y, pz, c))

    def dz(d):
        pz = lax.rem(z + d, 8)
        return remote(pc.at[0, c, :, pz // 2, pz % 2], rzd.at[d - 1], dzs.at[d - 1], dzr.at[d - 1], at(x, y, pz, c))

    def dy(d):
        py = lax.rem(y + d, 4)
        return remote(sd.at[py], ryd.at[d - 1], dys.at[d - 1], dyr.at[d - 1], at(x, py, z, c))

    def deliver(n):
        dev, src, dst, sem = outgoing[n]
        return remote(src, dst, fs.at[n], sem, dev)

    def send_out(n):
        dev, src, dst, _ = outgoing[n]

        @pl.when(jnp.logical_not(is_me(dev)))
        def _():
            deliver(n).start()

        if n < 2:
            @pl.when(is_me(dev))
            def _():
                dst[...] = src[...]

    def f_piece(p, k):
        whole(p, k).wait_recv()
        turn(xfull, 1, p)
        rows = pl.ds(pl.multiple_of(p * 128, 128), 128)
        value = dot3(gg[0, 0], gg[0, 1], gg[1, 0, rows, :], gg[1, 1, rows, :], NT_DIMS)
        for m in range(4):
            pf[m, p] = value[m * 128:(m + 1) * 128].reshape(2, 64, 128)
        for d in (2, 1, 3):
            fy(d, p).start()

    for k in range(2):
        value = half_of(peers[k])
        for q in range(6):
            hb[k, q] = chunk(value, q)
        swap(k).start()
    value = half_of(i)
    for q in range(6):
        blk[q, i] = chunk(value, q)
    whole(i, 3).start()
    value = half_of(peers[2])
    for q in range(6):
        hb[2, q] = chunk(value, q)
    swap(2).start()
    turn(blk, 0, i)
    swap_in(2).wait_recv()
    whole(peers[2], 2).start()
    turn(blk, 0, peers[2])
    swap_in(0).wait_recv()
    whole(peers[0], 0).start()
    part_way(i, 3).start()
    part_way(peers[2], 2).start()
    turn(blk, 0, peers[0])
    swap_in(1).wait_recv()
    whole(peers[1], 1).start()
    part_way(peers[0], 0).start()
    part_way(peers[1], 1).start()
    turn(blk, 0, peers[1])
    f_piece(i, 3)
    f_piece(peers[2], 2)
    f_piece(peers[0], 0)
    square(0, gg, 0, 0)
    core_swap(0).start()
    f_piece(peers[1], 1)
    core_sum(0)
    for d in (4, 3, 5, 2, 6, 1, 7):
        dz(d).start()
    turn_half(xfull, 3 * others, 1 - c)
    pieces = [(i, 3), (peers[2], 2), (peers[0], 0), (peers[1], 1)]
    for p, k in pieces:
        part_way(p, k).wait_recv()
    turn_half(xhalf, 0, c)
    square(1, eh, 0, 1)
    core_swap(1).start()
    for p, k in pieces:
        for d in (1, 2, 3):
            fy(d, p).wait_recv()
        sf[pl.ds(2 * p, 2)] = pf[y, p] + ryf[0, p] + ryf[1, p] + ryf[2, p]
    for d in (4, 3, 5, 2, 6, 1, 7):
        fz(d).start()
    core_sum(1)
    for d in (2, 1, 3):
        ey(d).start()
    for d in range(1, 8):
        dz(d).wait_recv()
    total = pc[0, c, :, z // 2, z % 2]
    for d in range(7):
        total = total + rzd[d]
    sd[...] = total
    for d in (2, 1, 3):
        dy(d).start()
    for d in (1, 2, 3):
        ey(d).wait_recv()
    se_[...] = pc[1, c, y] + rye[0] + rye[1] + rye[2]
    for d in (4, 3, 5, 2, 6, 1, 7):
        ez(d).start()
    for d in range(1, 8):
        fz(d).wait_recv()
    total = sf[z]
    for d in range(7):
        total = total + rzf[d]
    redf[...] = total
    send_out(1)
    send_out(2)
    for d in (1, 2, 3):
        dy(d).wait_recv()
    redq[0] = sd[y] + ryd[0] + ryd[1] + ryd[2]
    send_out(0)
    for d in range(1, 8):
        ez(d).wait_recv()
    total = se_[z // 2, z % 2]
    for d in range(7):
        total = total + rze[d]
    redq[1] = total
    send_out(3)
    send_out(4)

    for there, dev, dst, sem, src in incoming:
        @pl.when(there & jnp.logical_not(is_me(dev)))
        def _():
            remote(src, dst, fs.at[0], sem, (a, r)).wait_recv()

    @pl.when(delta == 0)
    def _():
        out_ref[...] = fin_q[0].reshape(128, 128)

    @pl.when(turned)
    def _():
        out_ref[...] = fin_q[0].reshape(128, 128) + fin_q[1].reshape(128, 128).T

    @pl.when(odd)
    def _():
        out_ref[...] = fin_f[0].reshape(128, 128) + fin_f[1].reshape(128, 128).T

    def drain(d, _):
        c1(d).wait_send()
        ti(d).wait_send()
        c2(d).wait_send()
        return 0

    lax.fori_loop(1, 16, drain, 0)
    for k in range(3):
        swap(k).wait_send()
    for n in range(2):
        core_swap(n).wait_send()
    for p, k in pieces:
        whole(p, k).wait_send()
        part_way(p, k).wait_send()
        for d in (1, 2, 3):
            fy(d, p).wait_send()
    for d in (1, 2, 3):
        ey(d).wait_send()
        dy(d).wait_send()
    for d in range(1, 8):
        fz(d).wait_send()
        ez(d).wait_send()
        dz(d).wait_send()
    for n in range(5):
        @pl.when(jnp.logical_not(is_me(outgoing[n][0])))
        def _():
            deliver(n).wait_send()


def on_device(three_index, coefficients, tile_index):
    dma = pltpu.SemaphoreType.DMA
    vm = pltpu.VMEM
    return pl.pallas_call(
        kernel,
        out_shape=jax.ShapeDtypeStruct((128, 128), F32),
        in_specs=[
            pl.BlockSpec(memory_space=pl.ANY),
            pl.BlockSpec(memory_space=pltpu.VMEM),
            pl.BlockSpec(memory_space=pltpu.SMEM),
        ],
        out_specs=pl.BlockSpec(memory_space=pltpu.VMEM),
        scratch_shapes=[
            vm((1536, 512), F32), vm((1536, 512), BF16), vm((1536, 512), BF16),
            vm((16, 8, 256), F32), vm((8, 128), jnp.int32), vm((16, 8, 128), jnp.int32),
            pltpu.SMEM((16, 128), jnp.int32),
            vm((15, 4, 8, 256), F32), vm((4, 16, 8, 256), F32),
            vm((512, 256), BF16), vm((512, 256), BF16),
            vm((3, 6, 128, 128), F32), vm((6, 4, 128, 128), F32), vm((6, 4, 128, 128), F32), vm((3, 4, 128, 128), F32),
            vm((2, 2, 512, 768), BF16), vm((2, 2, 512, 384), BF16),
            vm((2, 2, 4, 4, 2, 32, 128), F32), vm((2, 4, 4, 2, 32, 128), F32),
            vm((4, 4, 2, 64, 128), F32), vm((3, 4, 2, 64, 128), F32), vm((8, 64, 128), F32), vm((7, 64, 128), F32),
            vm((64, 128), F32),
            vm((3, 4, 2, 32, 128), F32), vm((4, 2, 32, 128), F32), vm((7, 32, 128), F32),
            vm((7, 4, 32, 128), F32), vm((4, 32, 128), F32), vm((3, 32, 128), F32),
            vm((2, 32, 128), F32), vm((2, 2, 2, 32, 128), F32), vm((2, 2, 64, 128), F32),
            dma((4,)), dma((15,)), dma((15,)), dma((15,)), dma((15,)), dma((15,)), dma((15,)), dma,
            dma((3,)), dma((3,)), dma((4, 2)), dma((4, 2)), dma((2,)), dma((2,)),
            dma((4, 3)), dma((4, 3)), dma((7,)), dma((7,)),
            dma((3,)), dma((3,)), dma((7,)), dma((7,)), dma((3,)), dma((3,)), dma((7,)), dma((7,)),
            dma((5,)), dma((2, 2, 2)), dma((2, 2)),
        ],
        compiler_params=pltpu.CompilerParams(
            collective_id=0, has_side_effects=True, vmem_limit_bytes=56 * 2**20
        ),
    )(three_index.reshape(1536, 512), coefficients.reshape(16, 8, 256), tile_index)


def solution(mesh):
    return jax.shard_map(
        on_device,
        mesh=mesh,
        in_specs=(P("aux", "row", None), P("aux", None), P("aux", "row", None)),
        out_specs=P("row", "aux"),
        check_vma=False,
    )
```

time: 110 us -> 92.6 us (0.84)
  the two profiles are of different devices: /device:TPU:18 before, /device:TPU:56 now
where the time goes in v2:
time: 92.6 us; the launch traced here: 90.8 us
  Pallas kernels  89.3 us (96%)
  local copies, waits for them, and re-layouts  1.47 us (2%)
    pallas_call x1, Pallas kernels, on_device(): pl.pallas_call(kernel, out_shape=jax.ShapeDtypeStruct((128, 128), F32), i...  89.3 us

profile of v2, /device:TPU:56, one launch (start us, length us, event | category | flops | bytes accessed | tf_op | source)
XLA Modules:
  0.0 90.8 jit_solution(8535990562325676382)
XLA Ops:
  0.0 89.3 %shard_map.37 = f32[128,128]{1,0:T(8,128)} custom-call(f32[1536,512]{1,0:T(8,128)} %bitcast.2, f32[16,8,256]{2,1,0:T(8,128)} %bitcast.3, s32[1,1,4]{2,1,0:T(1,128)} %t_ref.1), custom_call_target="tpu_custom_call" | custom-call | tf_op jit(solution)/shard_map/pallas_call | solution.py:432
  89.3 1.5 %copy.5 = f32[128,128]{1,0:T(8,128)} copy(f32[128,128]{1,0:T(8,128)} %shard_map.37) | data formatting | bytes 131072

commit v3 on v2

v3 whole, which is shorter than its diff:
```python
import functools

import jax
import jax.numpy as jnp
from jax import lax
from jax.experimental import pallas as pl
from jax.experimental.pallas import tpu as pltpu
from jax.sharding import PartitionSpec as P

MESH = pl.DeviceIdType.MESH
F32 = jnp.float32
BF16 = jnp.bfloat16
NT_DIMS = (((1,), (1,)), ((), ()))
NN_DIMS = (((1,), (0,)), ((), ()))


def split(value):
    high = value.astype(BF16)
    return high, (value - high.astype(F32)).astype(BF16)


def dot3(lh, ll, rh, rl, dims):
    dot = functools.partial(lax.dot_general, dimension_numbers=dims, preferred_element_type=F32)
    return dot(lh, rh) + (dot(lh, rl) + dot(ll, rh))


def kernel(
    x_ref, c_ref, t_ref, out_ref,
    xv, xh, xl, tslice, tvec, tall, tsm, picks, csel, ch, cl,
    hb, blk, xfull, xhalf, gg, eh,
    pc, cb, pf, ryf, sf, rzf, redf, rye, se_, rze, rzd, sd, ryd, redq, fin_q, fin_f,
    loads, c1s, c1r, tis, tir, c2s, c2r, tsem, has, har, xs, xr, ccs, ccr,
    fys, fyr, fzs, fzr, eys, eyr, ezs, ezr, dys, dyr, dzs, dzr, fs, frq, frf,
):
    a = lax.axis_index("aux")
    r = lax.axis_index("row")
    lo, z = a // 8, a % 8
    x, i = r // 4, r % 4
    hi, c = i // 2, i % 2
    y = hi * 2 + lo

    def at(px, py, pz, pc):
        return (py % 2) * 8 + pz, px * 4 + (py // 2) * 2 + pc

    def remote(src, dst, ss, rs, dev):
        return pltpu.make_async_remote_copy(
            src_ref=src, dst_ref=dst, send_sem=ss, recv_sem=rs, device_id=dev, device_id_type=MESH
        )

    def took(sem, ref):
        remote(ref, ref, sem, sem, (a, r)).wait_recv()

    def is_me(dev):
        return (dev[0] == a) & (dev[1] == r)

    def load_x(n):
        return pltpu.make_async_copy(x_ref.at[pl.ds(n * 384, 384)], xv.at[pl.ds(n * 384, 384)], loads)

    for n in range(4):
        load_x(n).start()

    sub = z % 2
    bi, bj = y, z // 2
    step = 2 * c - 1
    x_to = lax.rem(x + 4 + step, 4)
    x_back = lax.rem(x + 4 - step, 4)
    ea, eb = lax.rem(x + 3, 4), lax.rem(x + 1, 4)
    outgoing = [
        ((x * 4 + bj, x * 4 + bi), redq.at[0], fin_q.at[0, c, sub], frq.at[0]),
        ((x_back * 4 + bj, x * 4 + bi), redf, fin_f.at[0, sub], frf.at[0]),
        ((x * 4 + bi, x_back * 4 + bj), redf, fin_f.at[1, sub], frf.at[1]),
        ((eb * 4 + bj, ea * 4 + bi), redq.at[1], fin_q.at[0, c, sub], frq.at[0]),
        ((ea * 4 + bi, eb * 4 + bj), redq.at[1], fin_q.at[1, c, sub], frq.at[1]),
    ]
    xc = a // 4
    delta = lax.rem(xc + 4 - x, 4)
    odd = (delta % 2) == 1
    turned = delta == 2

    barrier = pltpu.get_barrier_semaphore()

    def greet(dev):
        pl.semaphore_signal(barrier, inc=1, device_id=dev, device_id_type=MESH)

    def greet_axes(d, _):
        greet((a, lax.rem(r + d, 16)))
        greet((lax.rem(a + d, 16), r))
        return 0

    lax.fori_loop(1, 16, greet_axes, 0)
    lane = lax.broadcasted_iota(jnp.int32, (8, 128), 1)
    ids = jnp.zeros((8, 128), jnp.int32)
    for s in range(4):
        ids = jnp.where(lane == s, t_ref[0, 0, s], ids)
    tvec[...] = ids
    pl.semaphore_wait(barrier, 30)

    def c1(d):
        return remote(c_ref.at[r], tslice.at[a], c1s, c1r, (lax.rem(a + d, 16), r))

    def ti(d):
        return remote(tvec, tall.at[r], tis, tir, (a, lax.rem(r + d, 16)))

    def start1(d, _):
        c1(d).start()
        ti(d).start()
        return 0

    lax.fori_loop(1, 16, start1, 0)
    tslice[a] = c_ref[r]
    tall[r] = ids

    def split_x(n, _):
        rows = pl.ds(pl.multiple_of(n * 128, 128), 128)
        high, low = split(xv[rows, :])
        xh[rows, :] = high
        xl[rows, :] = low
        return 0

    pltpu.make_async_copy(x_ref, xv, loads).wait()
    lax.fori_loop(0, 12, split_x, 0)

    took(tir, tall.at[pl.ds(0, 15)])
    to_smem = pltpu.make_async_copy(tall.at[:, 0], tsm, tsem)
    to_smem.start()
    to_smem.wait()

    took(c1r, tslice.at[pl.ds(0, 15)])

    def c2(n, d):
        return remote(picks.at[d - 1, n], csel.at[n, :, r], c2s, c2r.at[n], (a, lax.rem(r + d, 16)))

    for n in range(2):
        def start2(d, _):
            who = lax.rem(r + d, 16)
            for s in range(4):
                picks[d - 1, n, s] = tslice[tsm[who, s], :, n * 128:(n + 1) * 128]
            c2(n, d).start()
            return 0

        lax.fori_loop(1, 16, start2, 0)
    for n in range(2):
        for s in range(4):
            csel[n, s, r] = tslice[tsm[r, s], :, n * 128:(n + 1) * 128]

    def take_c(n):
        took(c2r.at[n], picks.at[:, n])
        cols = slice(n * 128, (n + 1) * 128)
        for s in range(4):
            high, low = split(csel[n, s].reshape(128, 128))
            ch[s * 128:(s + 1) * 128, cols] = high
            cl[s * 128:(s + 1) * 128, cols] = low

    peers = [lax.rem(i + 2, 4), 3 - i, i + 1 - 2 * c]

    def swap(k, n):
        return remote(hb.at[k, pl.ds(3 * n, 3)], blk.at[pl.ds(3 * n, 3), i], has, har.at[2 * k + n], (a, x * 4 + peers[k]))

    def swap_in(k, n):
        return remote(hb.at[k, pl.ds(3 * n, 3)], blk.at[pl.ds(3 * n, 3), peers[k]], has, har.at[2 * k + n], (a, r))

    def half_of(g, n):
        rows = pl.ds(pl.multiple_of(g * 384, 128), 384)
        cols = slice(n * 128, (n + 1) * 128)
        return dot3(xh[rows, :], xl[rows, :], ch[:, cols], cl[:, cols], NN_DIMS).reshape(3, 128, 128)

    def turn(src, slot, p):
        rows = pl.ds(pl.multiple_of(p * 128, 128), 128)
        for q in range(6):
            high, low = split(src[q, p])
            gg[slot, 0, rows, q * 128:(q + 1) * 128] = high
            gg[slot, 1, rows, q * 128:(q + 1) * 128] = low

    def turn_half(src, start, slot):
        def body(n, _):
            rows = pl.ds(pl.multiple_of(n * 128, 128), 128)
            for q in range(3):
                high, low = split(src[start + q, n])
                eh[slot, 0, rows, q * 128:(q + 1) * 128] = high
                eh[slot, 1, rows, q * 128:(q + 1) * 128] = low
            return 0
        lax.fori_loop(0, 4, body, 0)

    mine = x // 2
    others = x_to // 2

    def whole(p, k, n):
        part = pl.ds(3 * n, 3)
        return remote(blk.at[part, p], xfull.at[part, p], xs.at[0], xr.at[2 * k + n], (a, x_to * 4 + i))

    def part_way(p):
        return remote(blk.at[pl.ds(3 * mine, 3), p], xhalf.at[:, p], xs.at[1], xr.at[8], (a, x_back * 4 + i))

    def get_whole(p, k):
        for n in range(2):
            whole(p, k, n).wait_recv()
        turn(xfull, 1, p)

    def square(n, buf, left, right):
        for jj in range(2):
            cols = slice(jj * 256, (jj + 1) * 256)
            value = dot3(buf[left, 0], buf[left, 1], buf[right, 0, cols, :], buf[right, 1, cols, :], NT_DIMS)
            for m in range(4):
                for jl in range(2):
                    for h in range(2):
                        pc[n, h, m, 2 * jj + jl] = value[
                            m * 128 + h * 64:m * 128 + (h + 1) * 64, jl * 128:(jl + 1) * 128
                        ].reshape(2, 32, 128)

    def core_swap(n):
        return remote(pc.at[n, 1 - c], cb.at[n], ccs, ccr.at[n], (a, r + 1 - 2 * c))

    def core_sum(n):
        core_swap(n).wait_recv()
        for m in range(4):
            pc[n, c, m] = pc[n, c, m] + cb[n, m]

    def fy(d, p):
        py = lax.rem(y + d, 4)
        return remote(pf.at[py, p], ryf.at[d - 1, p], fys, fyr, at(x, py, z, c))

    def fz(d):
        pz = lax.rem(z + d, 8)
        return remote(sf.at[pz], rzf.at[d - 1], fzs, fzr, at(x, y, pz, c))

    def ey(d):
        py = lax.rem(y + d, 4)
        return remote(pc.at[1, c, py], rye.at[d - 1], eys, eyr, at(x, py, z, c))

    def ez(d):
        pz = lax.rem(z + d, 8)
        return remote(se_.at[pz // 2, pz % 2], rze.at[d - 1], ezs, ezr, at(x, y, pz, c))

    def d_own(pz):
        return pc.at[0, c, :, pz // 2, pz % 2]

    def dz(d):
        pz = lax.rem(z + d, 8)
        return remote(d_own(pz), rzd.at[d - 1], dzs, dzr, at(x, y, pz, c))

    def dy(d):
        py = lax.rem(y + d, 4)
        return remote(sd.at[py], ryd.at[d - 1], dys, dyr, at(x, py, z, c))

    def deliver(n):
        dev, src, dst, sem = outgoing[n]
        return remote(src, dst, fs.at[n], sem, dev)

    def send_out(n):
        dev, src, dst, _ = outgoing[n]

        @pl.when(jnp.logical_not(is_me(dev)))
        def _():
            deliver(n).start()

        if n < 2:
            @pl.when(is_me(dev))
            def _():
                pltpu.make_async_copy(src, dst, outgoing[n][3]).start()

    def f_piece(p, k):
        get_whole(p, k)
        rows = pl.ds(pl.multiple_of(p * 128, 128), 128)
        value = dot3(gg[0, 0], gg[0, 1], gg[1, 0, rows, :], gg[1, 1, rows, :], NT_DIMS)
        for m in range(4):
            pf[m, p] = value[m * 128:(m + 1) * 128].reshape(2, 64, 128)
        for d in (2, 1, 3):
            fy(d, p).start()

    pair = hi * 2

    def f_row(m):
        rows = pl.ds(pl.multiple_of(m * 128, 128), 128)
        cols = pl.ds(pl.multiple_of(pair * 128, 256), 256)
        value = dot3(gg[0, 0, rows, :], gg[0, 1, rows, :], gg[1, 0, cols, :], gg[1, 1, cols, :], NT_DIMS)
        for n in range(2):
            pf[m, pair + n] = value[:, n * 128:(n + 1) * 128].reshape(2, 64, 128)
        d = lax.rem(m + 4 - y, 4)

        @pl.when(d > 0)
        def _():
            for n in range(2):
                fy(d, pair + n).start()

    def half_out(k, n):
        hb[k, 3 * n:3 * n + 3] = half_of(peers[k], n)
        swap(k, n).start()

    def half_own(n):
        blk[3 * n:3 * n + 3, i] = half_of(i, n)
        whole(i, 3, n).start()

    def arrived(k, n):
        swap_in(k, n).wait_recv()
        whole(peers[k], k, n).start()

    take_c(0)
    half_out(0, 0)
    half_own(0)
    half_out(2, 0)
    half_out(1, 0)
    take_c(1)
    half_out(0, 1)
    half_own(1)
    arrived(2, 0)
    half_out(2, 1)
    half_out(1, 1)
    turn(blk, 0, i)
    arrived(2, 1)
    turn(blk, 0, peers[2])
    arrived(0, 0)
    get_whole(i, 3)
    get_whole(peers[2], 2)
    part_way(i).start()
    part_way(peers[2]).start()
    f_row(i)
    f_row(peers[2])
    arrived(1, 0)
    arrived(0, 1)
    turn(blk, 0, peers[0])
    part_way(peers[0]).start()
    f_row(peers[0])
    arrived(1, 1)
    turn(blk, 0, peers[1])
    part_way(peers[1]).start()
    square(0, gg, 0, 0)
    core_swap(0).start()
    f_row(peers[1])
    core_sum(0)
    for d in (4, 3, 5, 2, 6, 1, 7):
        dz(d).start()
    f_piece(peers[0], 0)
    f_piece(peers[1], 1)
    turn_half(xfull, 3 * others, 1 - c)
    took(xr.at[8], xhalf)
    turn_half(xhalf, 0, c)
    square(1, eh, 0, 1)
    core_swap(1).start()
    core_sum(1)
    for d in (2, 1, 3):
        ey(d).start()
    took(fyr, ryf)
    for m in range(4):
        sf[2 * m:2 * m + 2] = pf[y, m] + ryf[0, m] + ryf[1, m] + ryf[2, m]
    for d in (4, 3, 5, 2, 6, 1, 7):
        fz(d).start()
    took(eyr, rye)
    se_[...] = pc[1, c, y] + rye[0] + rye[1] + rye[2]
    for d in (4, 3, 5, 2, 6, 1, 7):
        ez(d).start()
    took(dzr, rzd)
    total = d_own(z)[...]
    for d in range(7):
        total = total + rzd[d]
    sd[...] = total
    for d in (2, 1, 3):
        dy(d).start()
    took(fzr, rzf)
    total = sf[z]
    for d in range(7):
        total = total + rzf[d]
    redf[...] = total
    send_out(1)
    send_out(2)
    took(dyr, ryd)
    redq[0] = sd[y] + ryd[0] + ryd[1] + ryd[2]
    send_out(0)
    took(ezr, rze)
    total = se_[z // 2, z % 2]
    for d in range(7):
        total = total + rze[d]
    redq[1] = total
    send_out(3)
    send_out(4)

    @pl.when(delta == 0)
    def _():
        took(frq.at[0], fin_q.at[0])
        out_ref[...] = fin_q[0].reshape(128, 128)

    @pl.when(turned)
    def _():
        took(frq.at[0], fin_q.at[0])
        took(frq.at[1], fin_q.at[1])
        out_ref[...] = fin_q[0].reshape(128, 128) + fin_q[1].reshape(128, 128).T

    @pl.when(odd)
    def _():
        took(frf.at[0], fin_f.at[0])
        took(frf.at[1], fin_f.at[1])
        out_ref[...] = fin_f[0].reshape(128, 128) + fin_f[1].reshape(128, 128).T

    for sem, ref in (
        (c1s, tslice.at[pl.ds(0, 15)]), (tis, tall.at[pl.ds(0, 15)]), (c2s, picks), (has, hb),
        (xs.at[0], blk), (xs.at[1], xhalf), (ccs, cb), (fys, ryf), (fzs, rzf), (eys, rye), (ezs, rze), (dzs, rzd), (dys, ryd),
    ):
        took(sem, ref)
    for n in range(5):
        @pl.when(jnp.logical_not(is_me(outgoing[n][0])))
        def _():
            deliver(n).wait_send()


def on_device(three_index, coefficients, tile_index):
    dma = pltpu.SemaphoreType.DMA
    vm = pltpu.VMEM
    return pl.pallas_call(
        kernel,
        out_shape=jax.ShapeDtypeStruct((128, 128), F32),
        in_specs=[
            pl.BlockSpec(memory_space=pl.ANY),
            pl.BlockSpec(memory_space=pltpu.VMEM),
            pl.BlockSpec(memory_space=pltpu.SMEM),
        ],
        out_specs=pl.BlockSpec(memory_space=pltpu.VMEM),
        scratch_shapes=[
            vm((1536, 512), F32), vm((1536, 512), BF16), vm((1536, 512), BF16),
            vm((16, 8, 256), F32), vm((8, 128), jnp.int32), vm((16, 8, 128), jnp.int32),
            pltpu.SMEM((16, 128), jnp.int32),
            vm((15, 2, 4, 8, 128), F32), vm((2, 4, 16, 8, 128), F32),
            vm((512, 256), BF16), vm((512, 256), BF16),
            vm((3, 6, 128, 128), F32), vm((6, 4, 128, 128), F32), vm((6, 4, 128, 128), F32), vm((3, 4, 128, 128), F32),
            vm((2, 2, 512, 768), BF16), vm((2, 2, 512, 384), BF16),
            vm((2, 2, 4, 4, 2, 32, 128), F32), vm((2, 4, 4, 2, 32, 128), F32),
            vm((4, 4, 2, 64, 128), F32), vm((3, 4, 2, 64, 128), F32), vm((8, 64, 128), F32), vm((7, 64, 128), F32),
            vm((64, 128), F32),
            vm((3, 4, 2, 32, 128), F32), vm((4, 2, 32, 128), F32), vm((7, 32, 128), F32),
            vm((7, 4, 32, 128), F32), vm((4, 32, 128), F32), vm((3, 32, 128), F32),
            vm((2, 32, 128), F32), vm((2, 2, 2, 32, 128), F32), vm((2, 2, 64, 128), F32),
            dma, dma, dma, dma, dma, dma, dma((2,)), dma,
            dma, dma((6,)), dma((2,)), dma((9,)), dma, dma((2,)),
            dma, dma, dma, dma, dma, dma, dma, dma, dma, dma, dma, dma,
            dma((5,)), dma((2,)), dma((2,)),
        ],
        compiler_params=pltpu.CompilerParams(
            collective_id=0, has_side_effects=True, vmem_limit_bytes=56 * 2**20
        ),
    )(three_index.reshape(1536, 512), coefficients.reshape(16, 8, 256), tile_index)


def solution(mesh):
    return jax.shard_map(
        on_device,
        mesh=mesh,
        in_specs=(P("aux", "row", None), P("aux", None), P("aux", "row", None)),
        out_specs=P("row", "aux"),
        check_vma=False,
    )
```

time: 92.6 us -> 81.3 us (0.88); the launches traced: 90.8 us -> 81 us
  Pallas kernels: 89.3 us -> 79.5 us
    pallas_call x1, Pallas kernels: 89.3 us -> 79.5 us  [on_device(): pl.pallas_call(kernel, out_shape=jax.ShapeDtypeStruct((128, 128), F32), i...]
where the time goes in v3:
time: 81.3 us; the launch traced here: 81 us
  Pallas kernels  79.5 us (98%)
  local copies, waits for them, and re-layouts  1.47 us (2%)
    pallas_call x1, Pallas kernels, on_device(): pl.pallas_call(kernel, out_shape=jax.ShapeDtypeStruct((128, 128), F32), i...  79.5 us

profile of v3, /device:TPU:56, one launch (start us, length us, event | category | flops | bytes accessed | tf_op | source)
XLA Modules:
  0.0 81.0 jit_solution(7011974623024134826)
XLA Ops:
  0.0 79.5 %shard_map.37 = f32[128,128]{1,0:T(8,128)} custom-call(f32[1536,512]{1,0:T(8,128)} %bitcast.2, f32[16,8,256]{2,1,0:T(8,128)} %bitcast.3, s32[1,1,4]{2,1,0:T(1,128)} %t_ref.1), custom_call_target="tpu_custom_call" | custom-call | tf_op jit(solution)/shard_map/pallas_call | solution.py:407
  79.5 1.5 %copy.5 = f32[128,128]{1,0:T(8,128)} copy(f32[128,128]{1,0:T(8,128)} %shard_map.37) | data formatting | bytes 131072

commit v4 on v3

--- a/solution.py
+++ b/solution.py
@@ -26,7 +26,7 @@
 
 def kernel(
     x_ref, c_ref, t_ref, out_ref,
-    xv, xh, xl, tslice, tvec, tall, tsm, picks, csel, ch, cl,
+    xv, xh, xl, tslice, tvec, tall, tsm, tloc, picks, csel, ch, cl,
     hb, blk, xfull, xhalf, gg, eh,
     pc, cb, pf, ryf, sf, rzf, redf, rye, se_, rze, rzd, sd, ryd, redq, fin_q, fin_f,
     loads, c1s, c1r, tis, tir, c2s, c2r, tsem, has, har, xs, xr, ccs, ccr,
@@ -53,8 +53,24 @@
     def is_me(dev):
         return (dev[0] == a) & (dev[1] == r)
 
+    barrier = pltpu.get_barrier_semaphore()
+
+    def greet(dev):
+        pl.semaphore_signal(barrier, inc=1, device_id=dev, device_id_type=MESH)
+
+    def greet_axes(d, _):
+        greet((a, lax.rem(r + d, 16)))
+        greet((lax.rem(a + d, 16), r))
+        return 0
+
+    lax.fori_loop(1, 16, greet_axes, 0)
+    own_c = pltpu.make_async_copy(c_ref.at[r], tslice.at[a], loads.at[1])
+    own_t = pltpu.make_async_copy(t_ref.at[0], tloc, loads.at[2])
+    own_t.start()
+    own_c.start()
+
     def load_x(n):
-        return pltpu.make_async_copy(x_ref.at[pl.ds(n * 384, 384)], xv.at[pl.ds(n * 384, 384)], loads)
+        return pltpu.make_async_copy(x_ref.at[pl.ds(n * 384, 384)], xv.at[pl.ds(n * 384, 384)], loads.at[0])
 
     for n in range(4):
         load_x(n).start()
@@ -77,26 +93,17 @@
     odd = (delta % 2) == 1
     turned = delta == 2
 
-    barrier = pltpu.get_barrier_semaphore()
-
-    def greet(dev):
-        pl.semaphore_signal(barrier, inc=1, device_id=dev, device_id_type=MESH)
-
-    def greet_axes(d, _):
-        greet((a, lax.rem(r + d, 16)))
-        greet((lax.rem(a + d, 16), r))
-        return 0
-
-    lax.fori_loop(1, 16, greet_axes, 0)
     lane = lax.broadcasted_iota(jnp.int32, (8, 128), 1)
+    own_t.wait()
     ids = jnp.zeros((8, 128), jnp.int32)
     for s in range(4):
-        ids = jnp.where(lane == s, t_ref[0, 0, s], ids)
+        ids = jnp.where(lane == s, tloc[0, s], ids)
     tvec[...] = ids
+    own_c.wait()
     pl.semaphore_wait(barrier, 30)
 
     def c1(d):
-        return remote(c_ref.at[r], tslice.at[a], c1s, c1r, (lax.rem(a + d, 16), r))
+        return remote(tslice.at[a], tslice.at[a], c1s, c1r, (lax.rem(a + d, 16), r))
 
     def ti(d):
         return remote(tvec, tall.at[r], tis, tir, (a, lax.rem(r + d, 16)))
@@ -107,7 +114,6 @@
         return 0
 
     lax.fori_loop(1, 16, start1, 0)
-    tslice[a] = c_ref[r]
     tall[r] = ids
 
     def split_x(n, _):
@@ -117,7 +123,7 @@
         xl[rows, :] = low
         return 0
 
-    pltpu.make_async_copy(x_ref, xv, loads).wait()
+    pltpu.make_async_copy(x_ref, xv, loads.at[0]).wait()
     lax.fori_loop(0, 12, split_x, 0)
 
     took(tir, tall.at[pl.ds(0, 15)])
@@ -409,14 +415,14 @@
         out_shape=jax.ShapeDtypeStruct((128, 128), F32),
         in_specs=[
             pl.BlockSpec(memory_space=pl.ANY),
-            pl.BlockSpec(memory_space=pltpu.VMEM),
-            pl.BlockSpec(memory_space=pltpu.SMEM),
+            pl.BlockSpec(memory_space=pl.ANY),
+            pl.BlockSpec(memory_space=pl.ANY),
         ],
         out_specs=pl.BlockSpec(memory_space=pltpu.VMEM),
         scratch_shapes=[
             vm((1536, 512), F32), vm((1536, 512), BF16), vm((1536, 512), BF16),
             vm((16, 8, 256), F32), vm((8, 128), jnp.int32), vm((16, 8, 128), jnp.int32),
-            pltpu.SMEM((16, 128), jnp.int32),
+            pltpu.SMEM((16, 128), jnp.int32), pltpu.SMEM((1, 4), jnp.int32),
             vm((15, 2, 4, 8, 128), F32), vm((2, 4, 16, 8, 128), F32),
             vm((512, 256), BF16), vm((512, 256), BF16),
             vm((3, 6, 128, 128), F32), vm((6, 4, 128, 128), F32), vm((6, 4, 128, 128), F32), vm((3, 4, 128, 128), F32),
@@ -427,7 +433,7 @@
             vm((3, 4, 2, 32, 128), F32), vm((4, 2, 32, 128), F32), vm((7, 32, 128), F32),
             vm((7, 4, 32, 128), F32), vm((4, 32, 128), F32), vm((3, 32, 128), F32),
             vm((2, 32, 128), F32), vm((2, 2, 2, 32, 128), F32), vm((2, 2, 64, 128), F32),
-            dma, dma, dma, dma, dma, dma, dma((2,)), dma,
+            dma((3,)), dma, dma, dma, dma, dma, dma((2,)), dma,
             dma, dma((6,)), dma((2,)), dma((9,)), dma, dma((2,)),
             dma, dma, dma, dma, dma, dma, dma, dma, dma, dma, dma, dma,
             dma((5,)), dma((2,)), dma((2,)),

time: 81.3 us -> 80.1 us (0.985)
  Pallas kernels: 79.5 us -> 78.5 us
    pallas_call x1, Pallas kernels: 79.5 us -> 78.5 us  [on_device(): pl.pallas_call(kernel, out_shape=jax.ShapeDtypeStruct((128, 128), F32), i...]
where the time goes in v4:
time: 80.1 us; the launch traced here: 80 us
  Pallas kernels  78.5 us (98%)
  local copies, waits for them, and re-layouts  1.47 us (2%)
    pallas_call x1, Pallas kernels, on_device(): pl.pallas_call(kernel, out_shape=jax.ShapeDtypeStruct((128, 128), F32), i...  78.5 us

profile of v4, /device:TPU:56, one launch (start us, length us, event | category | flops | bytes accessed | tf_op | source)
XLA Modules:
  0.0 80.0 jit_solution(7830858980494711288)
XLA Ops:
  0.0 78.5 %shard_map.37 = f32[128,128]{1,0:T(8,128)} custom-call(f32[1536,512]{1,0:T(8,128)} %bitcast.2, f32[16,8,256]{2,1,0:T(8,128)} %bitcast.3, s32[1,1,4]{2,1,0:T(1,128)} %t_ref.1), custom_call_target="tpu_custom_call" | custom-call | tf_op jit(solution)/shard_map/pallas_call | solution.py:413
  78.5 1.5 %copy.5 = f32[128,128]{1,0:T(8,128)} copy(f32[128,128]{1,0:T(8,128)} %shard_map.37) | data formatting | bytes 131072

commit v5 on v4

--- a/solution.py
+++ b/solution.py
@@ -75,14 +75,20 @@
     for n in range(4):
         load_x(n).start()
 
-    sub = z % 2
-    bi, bj = y, z // 2
+    def owned(pz, side):
+        far = jnp.where(pz // 4 == side, 0, 1)
+        return jnp.where(far == 0, pz % 4, 3 - pz % 4), far
+
+    side = (x + 1) % 2
+    bi = y
+    bj, sub = owned(z, side)
+    dj, dsub = owned(z, 1 - side)
     step = 2 * c - 1
     x_to = lax.rem(x + 4 + step, 4)
     x_back = lax.rem(x + 4 - step, 4)
     ea, eb = lax.rem(x + 3, 4), lax.rem(x + 1, 4)
     outgoing = [
-        ((x * 4 + bj, x * 4 + bi), redq.at[0], fin_q.at[0, c, sub], frq.at[0]),
+        ((x * 4 + dj, x * 4 + bi), redq.at[0], fin_q.at[0, c, dsub], frq.at[0]),
         ((x_back * 4 + bj, x * 4 + bi), redf, fin_f.at[0, sub], frf.at[0]),
         ((x * 4 + bi, x_back * 4 + bj), redf, fin_f.at[1, sub], frf.at[1]),
         ((eb * 4 + bj, ea * 4 + bi), redq.at[1], fin_q.at[0, c, sub], frq.at[0]),
@@ -227,7 +233,8 @@
 
     def fz(d):
         pz = lax.rem(z + d, 8)
-        return remote(sf.at[pz], rzf.at[d - 1], fzs, fzr, at(x, y, pz, c))
+        j, f = owned(pz, side)
+        return remote(sf.at[2 * j + f], rzf.at[d - 1], fzs, fzr, at(x, y, pz, c))
 
     def ey(d):
         py = lax.rem(y + d, 4)
@@ -235,10 +242,12 @@
 
     def ez(d):
         pz = lax.rem(z + d, 8)
-        return remote(se_.at[pz // 2, pz % 2], rze.at[d - 1], ezs, ezr, at(x, y, pz, c))
+        j, f = owned(pz, side)
+        return remote(se_.at[j, f], rze.at[d - 1], ezs, ezr, at(x, y, pz, c))
 
     def d_own(pz):
-        return pc.at[0, c, :, pz // 2, pz % 2]
+        j, f = owned(pz, 1 - side)
+        return pc.at[0, c, :, j, f]
 
     def dz(d):
         pz = lax.rem(z + d, 8)
@@ -304,28 +313,28 @@
     half_out(0, 0)
     half_own(0)
     half_out(2, 0)
-    half_out(1, 0)
     take_c(1)
     half_out(0, 1)
     half_own(1)
     arrived(2, 0)
+    half_out(1, 0)
     half_out(2, 1)
     half_out(1, 1)
     turn(blk, 0, i)
     arrived(2, 1)
     turn(blk, 0, peers[2])
     arrived(0, 0)
+    arrived(0, 1)
+    turn(blk, 0, peers[0])
     get_whole(i, 3)
     get_whole(peers[2], 2)
     part_way(i).start()
     part_way(peers[2]).start()
     f_row(i)
     f_row(peers[2])
+    f_row(peers[0])
     arrived(1, 0)
-    arrived(0, 1)
-    turn(blk, 0, peers[0])
     part_way(peers[0]).start()
-    f_row(peers[0])
     arrived(1, 1)
     turn(blk, 0, peers[1])
     part_way(peers[1]).start()
@@ -362,7 +371,7 @@
     for d in (2, 1, 3):
         dy(d).start()
     took(fzr, rzf)
-    total = sf[z]
+    total = sf[2 * bj + sub]
     for d in range(7):
         total = total + rzf[d]
     redf[...] = total
@@ -372,7 +381,7 @@
     redq[0] = sd[y] + ryd[0] + ryd[1] + ryd[2]
     send_out(0)
     took(ezr, rze)
-    total = se_[z // 2, z % 2]
+    total = se_[bj, sub]
     for d in range(7):
         total = total + rze[d]
     redq[1] = total
@@ -439,7 +448,7 @@
             dma((5,)), dma((2,)), dma((2,)),
         ],
         compiler_params=pltpu.CompilerParams(
-            collective_id=0, has_side_effects=True, vmem_limit_bytes=56 * 2**20
+            collective_id=0, has_side_effects=True, vmem_limit_bytes=55091 * 2**10
         ),
     )(three_index.reshape(1536, 512), coefficients.reshape(16, 8, 256), tile_index)
 

time: 80.1 us -> 77.8 us (0.971)
  Pallas kernels: 78.5 us -> 76.4 us
    pallas_call x1, Pallas kernels: 78.5 us -> 76.4 us  [on_device(): pl.pallas_call(kernel, out_shape=jax.ShapeDtypeStruct((128, 128), F32), i...]
where the time goes in v5:
time: 77.8 us; the launch traced here: 77.7 us
  Pallas kernels  76.4 us (98%)
  local copies, waits for them, and re-layouts  1.29 us (2%)
    pallas_call x1, Pallas kernels, on_device(): pl.pallas_call(kernel, out_shape=jax.ShapeDtypeStruct((128, 128), F32), i...  76.4 us

profile of v5, /device:TPU:56, one launch (start us, length us, event | category | flops | bytes accessed | tf_op | source)
XLA Modules:
  0.0 77.7 jit_solution(14677858033689542196)
XLA Ops:
  0.0 0.0 copy-start
  0.0 0.7 copy-done
  0.7 76.4 %shard_map.37 = f32[128,128]{1,0:T(8,128)S(1)} custom-call(f32[1536,512]{1,0:T(8,128)} %bitcast.2, f32[16,8,256]{2,1,0:T(8,128)} %bitcast.3, s32[1,1,4]{2,1,0:T(1,128)S(1)} %copy-done), custom_call_target="tpu_custom_call" | custom-call | tf_op jit(solution)/shard_map/pallas_call | solution.py:422
  77.1 0.6 copy.5
Async XLA Ops:
  0.0 0.7 copy-start

commit v6 on v5

--- a/solution.py
+++ b/solution.py
@@ -176,9 +176,9 @@
         cols = slice(n * 128, (n + 1) * 128)
         return dot3(xh[rows, :], xl[rows, :], ch[:, cols], cl[:, cols], NN_DIMS).reshape(3, 128, 128)
 
-    def turn(src, slot, p):
+    def turn(src, slot, p, half=None):
         rows = pl.ds(pl.multiple_of(p * 128, 128), 128)
-        for q in range(6):
+        for q in range(6) if half is None else range(3 * half, 3 * half + 3):
             high, low = split(src[q, p])
             gg[slot, 0, rows, q * 128:(q + 1) * 128] = high
             gg[slot, 1, rows, q * 128:(q + 1) * 128] = low
@@ -274,11 +274,15 @@
                 pltpu.make_async_copy(src, dst, outgoing[n][3]).start()
 
     def f_piece(p, k):
-        get_whole(p, k)
         rows = pl.ds(pl.multiple_of(p * 128, 128), 128)
-        value = dot3(gg[0, 0], gg[0, 1], gg[1, 0, rows, :], gg[1, 1, rows, :], NT_DIMS)
-        for m in range(4):
-            pf[m, p] = value[m * 128:(m + 1) * 128].reshape(2, 64, 128)
+        for n in range(2):
+            whole(p, k, n).wait_recv()
+            turn(xfull, 1, p, n)
+            part = slice(n * 384, (n + 1) * 384)
+            value = dot3(gg[0, 0, :, part], gg[0, 1, :, part], gg[1, 0, rows, part], gg[1, 1, rows, part], NT_DIMS)
+            for m in range(4):
+                block = value[m * 128:(m + 1) * 128].reshape(2, 64, 128)
+                pf[m, p] = block if n == 0 else pf[m, p] + block
         for d in (2, 1, 3):
             fy(d, p).start()
 
@@ -304,6 +308,11 @@
     def half_own(n):
         blk[3 * n:3 * n + 3, i] = half_of(i, n)
         whole(i, 3, n).start()
+
+        @pl.when(mine == n)
+        def _():
+            part_way(i).start()
+
 
     def arrived(k, n):
         swap_in(k, n).wait_recv()
@@ -328,7 +337,6 @@
     turn(blk, 0, peers[0])
     get_whole(i, 3)
     get_whole(peers[2], 2)
-    part_way(i).start()
     part_way(peers[2]).start()
     f_row(i)
     f_row(peers[2])

time: 77.8 us -> 77.3 us (level); the launches traced: 77.7 us -> 75.8 us
  Pallas kernels: 76.4 us -> 74.5 us
    pallas_call x1, Pallas kernels: 76.4 us -> 74.5 us  [on_device(): pl.pallas_call(kernel, out_shape=jax.ShapeDtypeStruct((128, 128), F32), i...]
where the time goes in v6:
time: 77.3 us; the launch traced here: 75.8 us
  Pallas kernels  74.5 us (96%)
  local copies, waits for them, and re-layouts  1.29 us (2%)
    pallas_call x1, Pallas kernels, on_device(): pl.pallas_call(kernel, out_shape=jax.ShapeDtypeStruct((128, 128), F32), i...  74.5 us

profile of v6, /device:TPU:56, one launch (start us, length us, event | category | flops | bytes accessed | tf_op | source)
XLA Modules:
  0.0 75.8 jit_solution(17910981897172854291)
XLA Ops:
  0.0 0.0 copy-start
  0.0 0.7 copy-done
  0.7 74.5 %shard_map.37 = f32[128,128]{1,0:T(8,128)S(1)} custom-call(f32[1536,512]{1,0:T(8,128)} %bitcast.2, f32[16,8,256]{2,1,0:T(8,128)} %bitcast.3, s32[1,1,4]{2,1,0:T(1,128)S(1)} %copy-done), custom_call_target="tpu_custom_call" | custom-call | tf_op jit(solution)/shard_map/pallas_call | solution.py:430
  75.2 0.6 copy.5
Async XLA Ops:
  0.0 0.7 copy-start

commit v7 on v6

--- a/solution.py
+++ b/solution.py
@@ -10,6 +10,8 @@
 MESH = pl.DeviceIdType.MESH
 F32 = jnp.float32
 BF16 = jnp.bfloat16
+AUX_ORDER = (12, 4, 11, 13, 5, 3, 10, 14, 6, 2, 9, 15, 7, 1, 8)
+ROW_ORDER = (10, 6, 11, 9, 7, 8, 5, 2, 14, 13, 3, 12, 4, 15, 1)
 NT_DIMS = (((1,), (1,)), ((), ()))
 NN_DIMS = (((1,), (0,)), ((), ()))
 
@@ -58,12 +60,10 @@
     def greet(dev):
         pl.semaphore_signal(barrier, inc=1, device_id=dev, device_id_type=MESH)
 
-    def greet_axes(d, _):
+    for d in AUX_ORDER:
+        greet((lax.rem(a + d, 16), r))
+    for d in ROW_ORDER:
         greet((a, lax.rem(r + d, 16)))
-        greet((lax.rem(a + d, 16), r))
-        return 0
-
-    lax.fori_loop(1, 16, greet_axes, 0)
     own_c = pltpu.make_async_copy(c_ref.at[r], tslice.at[a], loads.at[1])
     own_t = pltpu.make_async_copy(t_ref.at[0], tloc, loads.at[2])
     own_t.start()
@@ -114,12 +114,10 @@
     def ti(d):
         return remote(tvec, tall.at[r], tis, tir, (a, lax.rem(r + d, 16)))
 
-    def start1(d, _):
+    for d in AUX_ORDER:
         c1(d).start()
+    for d in ROW_ORDER:
         ti(d).start()
-        return 0
-
-    lax.fori_loop(1, 16, start1, 0)
     tall[r] = ids
 
     def split_x(n, _):

time: 77.3 us -> 76.9 us (level); the launches traced: 75.8 us -> 76.5 us
  no operation moved by 1% of the time
where the time goes in v7:
time: 76.9 us; the launch traced here: 76.5 us
  Pallas kernels  75.2 us (98%)
  local copies, waits for them, and re-layouts  1.29 us (2%)
    pallas_call x1, Pallas kernels, on_device(): pl.pallas_call(kernel, out_shape=jax.ShapeDtypeStruct((128, 128), F32), i...  75.2 us

profile of v7, /device:TPU:56, one launch (start us, length us, event | category | flops | bytes accessed | tf_op | source)
XLA Modules:
  0.0 76.5 jit_solution(4015606758376242640)
XLA Ops:
  0.0 0.0 copy-start
  0.0 0.7 copy-done
  0.7 75.2 %shard_map.37 = f32[128,128]{1,0:T(8,128)S(1)} custom-call(f32[1536,512]{1,0:T(8,128)} %bitcast.2, f32[16,8,256]{2,1,0:T(8,128)} %bitcast.3, s32[1,1,4]{2,1,0:T(1,128)S(1)} %copy-done), custom_call_target="tpu_custom_call" | custom-call | tf_op jit(solution)/shard_map/pallas_call | solution.py:428
  75.9 0.6 copy.5
Async XLA Ops:
  0.0 0.7 copy-start

commit v8 on v7

--- a/solution.py
+++ b/solution.py
@@ -141,14 +141,11 @@
         return remote(picks.at[d - 1, n], csel.at[n, :, r], c2s, c2r.at[n], (a, lax.rem(r + d, 16)))
 
     for n in range(2):
-        def start2(d, _):
+        for d in ROW_ORDER:
             who = lax.rem(r + d, 16)
             for s in range(4):
                 picks[d - 1, n, s] = tslice[tsm[who, s], :, n * 128:(n + 1) * 128]
             c2(n, d).start()
-            return 0
-
-        lax.fori_loop(1, 16, start2, 0)
     for n in range(2):
         for s in range(4):
             csel[n, s, r] = tslice[tsm[r, s], :, n * 128:(n + 1) * 128]

time: 76.9 us -> 76.4 us (level)
  no operation moved by 1% of the time
where the time goes in v8:
time: 76.4 us; the launch traced here: 75.8 us
  Pallas kernels  74.5 us (98%)
  local copies, waits for them, and re-layouts  1.29 us (2%)
    pallas_call x1, Pallas kernels, on_device(): pl.pallas_call(kernel, out_shape=jax.ShapeDtypeStruct((128, 128), F32), i...  74.5 us

profile of v8, /device:TPU:56, one launch (start us, length us, event | category | flops | bytes accessed | tf_op | source)
XLA Modules:
  0.0 75.8 jit_solution(9609709133835231008)
XLA Ops:
  0.0 0.0 copy-start
  0.0 0.7 copy-done
  0.7 74.5 %shard_map.37 = f32[128,128]{1,0:T(8,128)S(1)} custom-call(f32[1536,512]{1,0:T(8,128)} %bitcast.2, f32[16,8,256]{2,1,0:T(8,128)} %bitcast.3, s32[1,1,4]{2,1,0:T(1,128)S(1)} %copy-done), custom_call_target="tpu_custom_call" | custom-call | tf_op jit(solution)/shard_map/pallas_call | solution.py:425
  75.2 0.6 copy.5
Async XLA Ops:
  0.0 0.7 copy-start
